TPU v7x, 512 devices: a whole 4x4x16 slice. The times are simulated.
512 devices in a mesh: pipe: 2 (over z_hi), ctx: 64 (over y, z_lo, core), tp: 4 (over x).
Axes of the slice: x: 4, y: 4, z: 16 (z_hi: 2, z_lo: 8; z = z_hi * 8 + z_lo), core: 2. Of those that a mesh axis runs over, the one named last changes fastest.
Arguments:
- section_output: bfloat16 [2, 8192, 8192], P('pipe', 'ctx', 'tp'), may hold values from -26 to 26
- norm_gain: float32 [2, 8192], P('pipe'), may hold values from 0.1 to 1.9
- kv_weight: bfloat16 [2, 8192, 1024], P('pipe', 'ctx', 'tp'), may hold values from -0.0625 to 0.0625
- queries: bfloat16 [2, 8192, 4096], P('pipe', 'ctx', 'tp'), may hold values from -171 to 171
- rank_block: int32 [128], replicated, may hold values from 0 to 127, each once
Outputs:
- attention: bfloat16 [2, 8192, 4096], P('pipe', 'ctx', 'tp')
- log_total: float32 [2, 8192, 32], P('pipe', 'ctx', 'tp')
Inputs may be any that keep to these rules, and one draw needn't show every extreme that they name: `rank_block`: each of 0 to 127 once.
All inputs are finite; a program needn't handle non-finite values.
Results may differ from a plain program's by a relative error of at most 0.017.
The roundings to bfloat16 on the way count: a program that leaves them out, or rounds other values in their place, can miss the bound.
Values may be sent and summed in bfloat16 or wider, within the bound.
No kernel may reach another device: no remote copies, remote signals or barrier semaphores. Data moves between devices by JAX's collectives and lax.ppermute only.
A program may use at most 128 MiB of HBM per device.

v0:
```python
import math
import jax
import jax.numpy as jnp
from jax import lax
from jax.sharding import PartitionSpec as P

HD = 128
norm_eps = 1e-05
rope_base = 500000.0
mask_fill = -1e30


def passed_along(shard, axis, by):
    peers = lax.axis_size(axis)
    return lax.ppermute(shard, axis, [(i, (i + by) % peers) for i in range(peers)])


def block_positions(rank_block, ctx_count, half_rows):
    block_ids = rank_block.reshape(ctx_count, 2)
    within = jnp.arange(half_rows, dtype=jnp.int32)
    return (block_ids[:, :, None] * half_rows + within[None, None, :]).reshape(-1)


def rotate_keys(raw_keys, positions):
    width = raw_keys.shape[-1]
    half_width = width // 2
    steps_f = jnp.arange(half_width, dtype=jnp.float32)
    inv_freq = jnp.exp(steps_f * (-2.0 / width) * math.log(rope_base))
    angles = positions.astype(jnp.float32)[:, None] * inv_freq[None, :]
    cosine = jnp.cos(angles)
    sine_part = jnp.sin(angles)
    first_half = raw_keys[:, :half_width]
    second_half = raw_keys[:, half_width:]
    return jnp.concatenate(
        [
            first_half * cosine - second_half * sine_part,
            second_half * cosine + first_half * sine_part,
        ],
        axis=1,
    )


def body(section_output, norm_gain, kv_weight, queries, rank_block):
    ctx_count = lax.axis_size("ctx")
    tok_rows = section_output.shape[1]
    half_rows = tok_rows // 2
    head_dim = HD
    head_count = queries.shape[2] // head_dim
    score_scale = 1.0 / math.sqrt(head_dim)
    received = passed_along(section_output, "pipe", 1)
    gathered = lax.all_gather(received, "tp", axis=2, tiled=True)[0].astype(jnp.float32)
    mean_sq = jnp.mean(gathered * gathered, axis=-1, keepdims=True)
    normed = (gathered * lax.rsqrt(mean_sq + norm_eps) * norm_gain[0]).astype(jnp.bfloat16)
    projected = jnp.dot(
        normed,
        lax.all_gather(kv_weight, "ctx", axis=1, tiled=True)[0],
        preferred_element_type=jnp.float32,
    )
    all_pos = block_positions(rank_block, ctx_count, half_rows)
    own_pos = lax.dynamic_slice_in_dim(all_pos, lax.axis_index("ctx") * tok_rows, tok_rows)
    keys = rotate_keys(projected[:, :head_dim], own_pos).astype(jnp.bfloat16)
    values = projected[:, head_dim:].astype(jnp.bfloat16)
    key_values = jnp.concatenate([keys, values], axis=1)
    query_rows = queries[0].reshape(tok_rows, head_count, head_dim)
    halves = (
        (query_rows[:half_rows], own_pos[:half_rows]),
        (query_rows[half_rows:], own_pos[half_rows:]),
    )

    def tile_logits(query_part, query_pos, segment, key_pos):
        logits = (
            jnp.einsum(
                "qhd,kd->hqk", query_part, segment[:, :head_dim], preferred_element_type=jnp.float32
            )
            * score_scale
        )
        allowed = key_pos[None, None, :] <= query_pos[None, :, None]
        return (logits, allowed)

    def weighted_sum(att_weights, segment):
        return jnp.einsum(
            "hqk,kd->qhd",
            att_weights,
            segment[:, head_dim:].astype(jnp.float32),
            precision=lax.Precision.HIGHEST,
        )

    start_pair = (
        jnp.full((head_count, half_rows), mask_fill, jnp.float32),
        jnp.zeros((head_count, half_rows), jnp.float32),
    )
    init_totals = (start_pair, start_pair)
    start_accum = jnp.zeros((half_rows, head_count, head_dim), jnp.float32)
    init_outputs = (start_accum, start_accum)
    segment = lax.all_gather(key_values, "ctx", axis=0, tiled=True)
    key_pos = all_pos
    results = []
    for half_idx in range(2):
        query_part, query_pos = halves[half_idx]

        def update(state_in, query_part=query_part, query_pos=query_pos):
            logits, allowed = tile_logits(query_part, query_pos, segment, key_pos)
            logits = jnp.where(allowed, logits, mask_fill)
            row_max = jnp.maximum(state_in[0], jnp.max(logits, axis=-1))
            row_sum = jnp.sum(jnp.exp(logits - row_max[..., None]), axis=-1)
            return (row_max, row_sum)

        results.append(update(init_totals[half_idx]))
    totals = tuple(results)
    log_halves = tuple((running_pair[0] + jnp.log(running_pair[1]) for running_pair in totals))
    output_segment = lax.all_gather(key_values, "ctx", axis=0, tiled=True)
    results = []
    for half_idx in range(2):
        query_part, query_pos = halves[half_idx]
        log_half = log_halves[half_idx]

        def update(accum, query_part=query_part, query_pos=query_pos, log_half=log_half):
            logits, allowed = tile_logits(query_part, query_pos, output_segment, all_pos)
            att_weights = jnp.where(allowed, jnp.exp(logits - log_half[..., None]), 0.0)
            return weighted_sum(att_weights, output_segment)

        results.append(update(init_outputs[half_idx]))
    outputs = tuple(results)
    attention = (
        jnp.concatenate(outputs, axis=0)
        .astype(jnp.bfloat16)
        .reshape(tok_rows, head_count * head_dim)
    )
    log_total = jnp.concatenate(
        [jnp.transpose(log_halves[0]), jnp.transpose(log_halves[1])], axis=0
    )
    return (attention[None], log_total[None])


def solution(mesh):
    return jax.shard_map(
        body,
        mesh=mesh,
        in_specs=(
            P("pipe", "ctx", "tp"),
            P("pipe", None),
            P("pipe", "ctx", "tp"),
            P("pipe", "ctx", "tp"),
            P(),
        ),
        out_specs=(P("pipe", "ctx", "tp"), P("pipe", "ctx", "tp")),
        check_vma=False,
    )
```

profile of v0, /device:TPU:1, one launch (start us, length us, event | category | flops | bytes accessed | tf_op | source)
XLA Modules:
  0.0 424.6 jit_solution(8950425790996297745)
XLA Ops:
  7.2 0.0 all-gather.4.cloned.1.call-start
  7.2 16.3 %collective-permute-start = (bf16[1,128,2048]{2,1,0:T(8,128)(2,1)}, bf16[1,128,2048]{2,1,0:T(8,128)(2,1)S(1)}, u32[]{:S(2)}, u32[]{:S(2)}) collective-permute-start(bf16[1,128,2048]{2,1,0:T(8,128)(2,1)} %param.5), channel_id=1, source_target_pairs={{0,256},{256,0},{1,257},{257,1},{2,258},{258,2},{3,259},{259,3},{4... | collective-permute-start | bytes 1572872 | tf_op jit(solution)/shard_map/ppermute | solution.py:15
  23.5 15.2 %collective-permute-done = bf16[1,128,2048]{2,1,0:T(8,128)(2,1)S(1)} collective-permute-done((bf16[1,128,2048]{2,1,0:T(8,128)(2,1)}, bf16[1,128,2048]{2,1,0:T(8,128)(2,1)S(1)}, u32[]{:S(2)}, u32[]{:S(2)}) %collective-permute-start) | collective-permute-done | bytes 524320 | tf_op jit(solution)/shard_map/ppermute | solution.py:15
  38.7 0.0 copy-start.1
  38.7 0.8 copy-done.1
  39.5 0.0 all-gather.4.cloned.1.call-update
  39.5 0.0 all-gather.6.cloned.1.call-start
  39.6 0.7 all-gather.6.cloned.1.call-update
  40.3 0.0 all-gather.8.cloned.1.call-start
  40.3 0.7 broadcast_multiply_fusion
  41.0 0.1 mul.100
  41.1 0.1 iota_add_fusion
  41.3 0.1 add.65
  41.4 0.1 fusion.57
  41.5 68.4 %all-gather.4.cloned.1.call-done = bf16[1,128,8192]{2,1,0:T(8,128)(2,1)} async-done(((bf16[1,128,2048]{2,1,0:T(8,128)(2,1)}), bf16[1,128,8192]{2,1,0:T(8,128)(2,1)}) %all-gather.4.cloned.1.call-update) | async-done | bytes 2097168 | tf_op jit(solution)/shard_map/all_gather | solution.py:51
  109.8 2.1 fusion.20
  111.9 123.5 %all-gather.6.cloned.1.call-done = bf16[1,8192,256]{2,1,0:T(8,128)(2,1)} async-done(((bf16[1,128,256]{2,1,0:T(8,128)(2,1)}), bf16[1,8192,256]{2,1,0:T(8,128)(2,1)}) %all-gather.6.cloned.1.call-update) | async-done | bytes 4194320 | tf_op jit(solution)/shard_map/all_gather | solution.py:56
  235.4 3.6 fusion.23
  239.0 0.1 fusion.58
  239.1 0.1 copy.20
  239.2 0.1 copy.19
  239.3 0.2 fusion.50
  239.5 0.1 copy.13
  239.6 0.1 copy.14
  239.7 0.7 pad_maximum_fusion.1
  240.5 0.0 all-gather.8.cloned.1.call-update
  240.5 1.0 slice_bitcast_fusion.15
  241.5 0.1 fusion.59
  241.6 0.6 broadcast_compare_fusion.1
  242.3 116.9 %all-gather.8.cloned.1.call-done = bf16[8192,256]{1,0:T(8,128)(2,1)} async-done(((bf16[128,256]{1,0:T(8,128)(2,1)}), bf16[8192,256]{1,0:T(8,128)(2,1)}) %all-gather.8.cloned.1.call-update) | async-done | bytes 4194320 | tf_op jit(solution)/shard_map/all_gather | solution.py:111
  359.2 0.0 copy-start.2
  359.2 9.1 %fusion.8 = (f32[8,64]{1,0:T(8,128)S(1)}, f32[8192,64,8]{0,1,2:T(8,128)}) fusion(pred[64,8192]{1,0:T(8,128)(4,1)S(1)} %get-tuple-element.10, bf16[64,8,128]{2,1,0:T(8,128)(2,1)S(1)} %bitcast.76, bf16[8192,256]{1,0:T(8,128)(2,1)} %all-gather.8.cloned.1.call-done), kind=kOutput, calls=%fused_computation.12 | convolution fusion | flops 1086324224 | bytes 19531776 | tf_op jit(solution)/shard_map/qhd,kd->hqk/dot_general | solution.py:72
  368.3 0.0 copy-done.2
  368.3 3.1 fusion.9
  371.4 0.0 copy-start
  371.4 16.4 %exponential_reduce_fusion = (f32[8,64]{1,0:T(8,128)S(1)}, f32[8,64]{1,0:T(8,128)S(1)}) fusion(f32[8192,64,8]{0,1,2:T(8,128)S(1)} %get-tuple-element.15, f32[8,64]{1,0:T(8,128)S(1)} %broadcast_maximum_fusion, pred[64,8192]{1,0:T(8,128)(4,1)S(1)} %get-tuple-element.11, f32[8,64]{1,0:T(8,128)S(1)} %broadcast_maximum_fusion.1, ...), kind=kLoop, calls=%fused_computation.10 | loop fusion | flops 33553408 | bytes 34611200 | tf_op jit(solution)/shard_map/reduce_sum | solution.py:105
  387.8 0.0 copy-done
  387.8 14.0 %fusion.40 = bf16[64,8,128]{2,0,1:T(8,128)(2,1)S(1)} fusion(f32[8192,64,8]{0,1,2:T(8,128)} %get-tuple-element.17, f32[8,64]{1,0:T(8,128)S(1)} %log_add_fusion.1, pred[64,8192]{1,0:T(8,128)(4,1)S(1)} %get-tuple-element.10, bf16[8192,256]{1,0:T(8,128)(2,1)S(1)} %copy-done.2), kind=kOutput, calls=%fused_computation.41 | convolution fusion | flops 6455099392 | bytes 19533824 | tf_op jit(solution)/shard_map/hqk,kd->qhd/dot_general | solution.py:81
  401.9 0.1 copy.16
  402.0 0.1 concatenate.25
  402.1 14.4 %fusion.37 = bf16[64,8,128]{2,0,1:T(8,128)(2,1)S(1)} fusion(f32[8192,64,8]{0,1,2:T(8,128)} %copy-done, f32[8,64]{1,0:T(8,128)S(1)} %log_add_fusion, pred[64,8192]{1,0:T(8,128)(4,1)S(1)} %get-tuple-element.11, bf16[8192,256]{1,0:T(8,128)(2,1)} %all-gather.8.cloned.1.call-done), kind=kOutput, calls=%fused_computation.40 | convolution fusion | flops 6455099392 | bytes 19531776 | tf_op jit(solution)/shard_map/hqk,kd->qhd/dot_general | solution.py:81
  416.5 0.1 copy.18
  416.6 0.1 concatenate.26
  416.7 0.7 pad_maximum_fusion
  417.4 0.7 maximum_bitcast_fusion
  (9 shorter events, 0.1 us)
Async XLA Ops:
  7.2 102.7 %all-gather.4.cloned.1.call-start = ((), (), s32[]{:S(2)}) async-start(), calls=%async_computation | async-start | bytes 2621440 | tf_op jit(solution)/shard_map/all_gather | solution.py:51
  7.2 31.5 %collective-permute-start = (bf16[1,128,2048]{2,1,0:T(8,128)(2,1)}, bf16[1,128,2048]{2,1,0:T(8,128)(2,1)S(1)}, u32[]{:S(2)}, u32[]{:S(2)}) collective-permute-start(bf16[1,128,2048]{2,1,0:T(8,128)(2,1)} %param.5), channel_id=1, source_target_pairs={{0,256},{256,0},{1,257},{257,1},{2,258},{258,2},{3,259},{259,3},{4... | collective-permute-start | bytes 1572872 | tf_op jit(solution)/shard_map/ppermute | solution.py:15
  38.7 0.8 copy-start.1
  39.5 195.9 %all-gather.6.cloned.1.call-start = ((), (), s32[]{:S(2)}) async-start(), calls=%async_computation.1 | async-start | bytes 4259840 | tf_op jit(solution)/shard_map/all_gather | solution.py:56
  40.3 318.9 %all-gather.8.cloned.1.call-start = ((), (), s32[]{:S(2)}) async-start(), calls=%async_computation.2 | async-start | bytes 4259840 | tf_op jit(solution)/shard_map/all_gather | solution.py:111
  359.2 9.1 %copy-start.2 = (bf16[8192,256]{1,0:T(8,128)(2,1)S(1)}, bf16[8192,256]{1,0:T(8,128)(2,1)}, u32[]{:S(2)}) copy-start(bf16[8192,256]{1,0:T(8,128)(2,1)} %all-gather.8.cloned.1.call-done) | copy-start | bytes 12582916
  371.4 16.4 %copy-start = (f32[8192,64,8]{0,1,2:T(8,128)}, f32[8192,64,8]{0,1,2:T(8,128)S(1)}, u32[]{:S(2)}) copy-start(f32[8192,64,8]{0,1,2:T(8,128)S(1)} %get-tuple-element.15) | copy-start | bytes 50331652
Sparse Core Ops, SparseCore 0:
  39.7 70.1 all-gather.3
  112.0 123.3 all-gather.5
  240.6 118.5 all-gather.7
where the time goes:
time: 425 us
  waiting for transfers between devices  325 us (76%)
  matrix products  44.3 us (10%)
  other arithmetic  22.4 us (5%)
  starting transfers between devices  16.4 us (4%)
  between operations  13.9 us (3%)
    all_gather x1, waiting for transfers between devices, body(): lax.all_gather(kv_weight, 'ctx', axis=1, tiled=True)[0]  123 us
    all_gather x1, waiting for transfers between devices, body(): output_segment = lax.all_gather(key_values, 'ctx', axis=0, tiled=True)  117 us
    all_gather x1, waiting for transfers between devices, body(): lax.all_gather(received, 'tp', axis=2, tiled=True)[0].astype(jnp.float32)  68.4 us
    dot_general x2, matrix products, weighted_sum(): jnp.einsum('hqk,kd->qhd', att_weights, segment[:, head_dim:].astype(jnp.f...  28.5 us
    reduce_sum x1, other arithmetic, update(): row_sum = jnp.sum(jnp.exp(logits - row_max[..., None]), axis=-1)  16.4 us
    ppermute x1, starting transfers between devices, passed_along(): lax.ppermute(shard, axis, [(i, (i + by) % peers) for i in range(peers)])  16.3 us
    ppermute x1, waiting for transfers between devices, passed_along(): lax.ppermute(shard, axis, [(i, (i + by) % peers) for i in range(peers)])  15.2 us
    dot_general x2, matrix products, tile_logits(): jnp.einsum('qhd,kd->hqk', query_part, segment[:, :head_dim], preferred_el...  12.2 us
  transfers between devices with their start and end apart: 4, of which 4 were waited for; matrix products, arithmetic and copies ran while one was open for 1% of the time, Pallas kernels for 0%

commit v1 on v0

--- a/solution.py
+++ b/solution.py
@@ -1,13 +1,25 @@
+import functools
 import math
 import jax
 import jax.numpy as jnp
 from jax import lax
 from jax.sharding import PartitionSpec as P
+from jax.lax import all_to_all, axis_size
 
 HD = 128
 norm_eps = 1e-05
 rope_base = 500000.0
 mask_fill = -1e30
+
+
+def wait_the_heads(mat, bus_axis):
+    copies = []
+    for _ in range(axis_size(bus_axis)):
+        copies.append(mat)
+    return jnp.concatenate(all_to_all(jnp.stack(copies, axis=0), bus_axis, 0, 0), axis=1)
+
+
+open_indices = functools.partial(wait_the_heads, bus_axis="ctx")
 
 
 def passed_along(shard, axis, by):
@@ -51,11 +63,7 @@
     gathered = lax.all_gather(received, "tp", axis=2, tiled=True)[0].astype(jnp.float32)
     mean_sq = jnp.mean(gathered * gathered, axis=-1, keepdims=True)
     normed = (gathered * lax.rsqrt(mean_sq + norm_eps) * norm_gain[0]).astype(jnp.bfloat16)
-    projected = jnp.dot(
-        normed,
-        lax.all_gather(kv_weight, "ctx", axis=1, tiled=True)[0],
-        preferred_element_type=jnp.float32,
-    )
+    projected = jnp.dot(normed, open_indices(kv_weight)[0], preferred_element_type=jnp.float32)
     all_pos = block_positions(rank_block, ctx_count, half_rows)
     own_pos = lax.dynamic_slice_in_dim(all_pos, lax.axis_index("ctx") * tok_rows, tok_rows)
     keys = rotate_keys(projected[:, :head_dim], own_pos).astype(jnp.bfloat16)

time: 425 us -> 480 us (1.13)
  waiting for transfers between devices: 325 us -> 369 us
  starting transfers between devices: 16.4 us -> 25.4 us
    all_gather x1 -> x0, waiting for transfers between devices: 123 us -> none  [body(): lax.all_gather(kv_weight, 'ctx', axis=1, tiled=True)[0]]
    ppermute x1, waiting for transfers between devices: 15.2 us -> 99.9 us  [passed_along(): lax.ppermute(shard, axis, [(i, (i + by) % peers) for i in range(peers)])]
    all_gather x1, waiting for transfers between devices: 68.4 us -> 147 us  [body(): lax.all_gather(received, 'tp', axis=2, tiled=True)[0].astype(jnp.float32)]
    all_to_all x0 -> x1, starting transfers between devices: none -> 17.4 us  [wait_the_heads(): all_to_all(jnp.stack(copies, axis=0), bus_axis, 0, 0)]
    ppermute x1, starting transfers between devices: 16.3 us -> 7.94 us  [passed_along(): lax.ppermute(shard, axis, [(i, (i + by) % peers) for i in range(peers)])]
    all_gather x1, waiting for transfers between devices: 117 us -> 123 us  [body(): output_segment = lax.all_gather(key_values, 'ctx', axis=0, tiled=True)]
  transfers between devices with their start and end apart: 4 -> 4, of which waited for: 4 -> 3; matrix products, arithmetic and copies ran while one was open for 1% -> 1% of each run, Pallas kernels for 0% -> 0%
where the time goes in v1:
time: 480 us
  waiting for transfers between devices  369 us (77%)
  matrix products  44.8 us (9%)
  starting transfers between devices  25.4 us (5%)
  other arithmetic  20.5 us (4%)
  between operations  14.3 us (3%)
  local copies, waits for them, and re-layouts  5.35 us (1%)
    all_gather x1, waiting for transfers between devices, body(): lax.all_gather(received, 'tp', axis=2, tiled=True)[0].astype(jnp.float32)  147 us
    all_gather x1, waiting for transfers between devices, body(): output_segment = lax.all_gather(key_values, 'ctx', axis=0, tiled=True)  123 us
    ppermute x1, waiting for transfers between devices, passed_along(): lax.ppermute(shard, axis, [(i, (i + by) % peers) for i in range(peers)])  99.9 us
    dot_general x2, matrix products, weighted_sum(): jnp.einsum('hqk,kd->qhd', att_weights, segment[:, head_dim:].astype(jnp.f...  28.7 us
    all_to_all x1, starting transfers between devices, wait_the_heads(): all_to_all(jnp.stack(copies, axis=0), bus_axis, 0, 0)  17.4 us
    reduce_sum x1, other arithmetic, update(): row_sum = jnp.sum(jnp.exp(logits - row_max[..., None]), axis=-1)  14.6 us
    dot_general x2, matrix products, tile_logits(): jnp.einsum('qhd,kd->hqk', query_part, segment[:, :head_dim], preferred_el...  12.6 us
  transfers between devices with their start and end apart: 4, of which 3 were waited for; matrix products, arithmetic and copies ran while one was open for 1% of the time, Pallas kernels for 0%

profile of v1, /device:TPU:1, one launch (start us, length us, event | category | flops | bytes accessed | tf_op | source)
XLA Modules:
  0.0 479.8 jit_solution(7184379556581599710)
XLA Ops:
  7.2 0.0 copy-start.2
  7.2 3.4 stack.2
  10.5 17.4 %all-to-all-start = ((bf16[64,1,128,256]{3,2,1,0:T(8,128)(2,1)}), bf16[64,1,128,256]{3,2,1,0:T(8,128)(2,1)}, u32[]{:S(2)}, u32[]{:S(2)}) async-start(bf16[64,1,128,256]{3,2,1,0:T(8,128)(2,1)} %stack.2), calls=%async_computation | async-start | bytes 8388608 | tf_op jit(solution)/shard_map/all_to_all | solution.py:19
  28.0 0.0 all-gather.3.cloned.1.call-start
  28.0 7.9 %collective-permute-start = (bf16[1,128,2048]{2,1,0:T(8,128)(2,1)}, bf16[1,128,2048]{2,1,0:T(8,128)(2,1)S(1)}, u32[]{:S(2)}, u32[]{:S(2)}) collective-permute-start(bf16[1,128,2048]{2,1,0:T(8,128)(2,1)} %param.5), channel_id=1, source_target_pairs={{0,256},{256,0},{1,257},{257,1},{2,258},{258,2},{3,259},{259,3},{4... | collective-permute-start | bytes 1572872 | tf_op jit(solution)/shard_map/ppermute | solution.py:27
  36.0 99.9 %collective-permute-done = bf16[1,128,2048]{2,1,0:T(8,128)(2,1)S(1)} collective-permute-done((bf16[1,128,2048]{2,1,0:T(8,128)(2,1)}, bf16[1,128,2048]{2,1,0:T(8,128)(2,1)S(1)}, u32[]{:S(2)}, u32[]{:S(2)}) %collective-permute-start) | collective-permute-done | bytes 524320 | tf_op jit(solution)/shard_map/ppermute | solution.py:27
  135.8 0.0 copy-start.1
  135.8 0.8 copy-done.1
  136.7 0.0 all-gather.3.cloned.1.call-update
  136.7 0.0 all-gather.5.cloned.1.call-start
  136.7 0.7 broadcast_multiply_fusion
  137.4 0.1 mul.100
  137.5 0.1 iota_add_fusion
  137.7 0.1 add.65
  137.8 0.1 fusion.56
  137.9 146.8 %all-gather.3.cloned.1.call-done = bf16[1,128,8192]{2,1,0:T(8,128)(2,1)} async-done(((bf16[1,128,2048]{2,1,0:T(8,128)(2,1)}), bf16[1,128,8192]{2,1,0:T(8,128)(2,1)}) %all-gather.3.cloned.1.call-update) | async-done | bytes 2097168 | tf_op jit(solution)/shard_map/all_gather | solution.py:63
  284.7 2.1 fusion.20
  286.8 0.0 all-to-all-done
  286.8 3.6 fusion.24
  290.4 0.1 fusion.57
  290.5 0.1 copy.20
  290.5 0.1 copy.19
  290.6 0.2 fusion.49
  290.9 0.1 copy.13
  291.0 0.1 copy.14
  291.1 0.7 pad_maximum_fusion.1
  291.8 0.0 all-gather.5.cloned.1.call-update
  291.9 0.0 copy-done.2
  291.9 0.1 fusion.58
  292.0 0.6 broadcast_compare_fusion.1
  292.7 122.7 %all-gather.5.cloned.1.call-done = bf16[8192,256]{1,0:T(8,128)(2,1)} async-done(((bf16[128,256]{1,0:T(8,128)(2,1)}), bf16[8192,256]{1,0:T(8,128)(2,1)}) %all-gather.5.cloned.1.call-update) | async-done | bytes 4194320 | tf_op jit(solution)/shard_map/all_gather | solution.py:119
  415.4 0.0 copy-start.3
  415.4 4.8 fusion.9
  420.2 0.0 copy-start
  420.2 0.0 copy-done.3
  420.2 7.8 %fusion.8 = (f32[8,64]{1,0:T(8,128)S(1)}, f32[8192,64,8]{0,1,2:T(8,128)}) fusion(pred[64,8192]{1,0:T(8,128)(4,1)S(1)} %get-tuple-element.10, bf16[64,8,128]{2,1,0:T(8,128)(2,1)S(1)} %bitcast.75, bf16[8192,256]{1,0:T(8,128)(2,1)S(1)} %copy-done.3), kind=kOutput, calls=%fused_computation.12 | convolution fusion | flops 1086324224 | bytes 19531776 | tf_op jit(solution)/shard_map/qhd,kd->hqk/dot_general | solution.py:80
  428.0 14.6 %exponential_reduce_fusion = (f32[8,64]{1,0:T(8,128)S(1)}, f32[8,64]{1,0:T(8,128)S(1)}) fusion(f32[8192,64,8]{0,1,2:T(8,128)S(1)} %get-tuple-element.15, f32[8,64]{1,0:T(8,128)S(1)} %broadcast_maximum_fusion, pred[64,8192]{1,0:T(8,128)(4,1)S(1)} %get-tuple-element.11, f32[8,64]{1,0:T(8,128)S(1)} %broadcast_maximum_fusion.1, ...), kind=kLoop, calls=%fused_computation.10 | loop fusion | flops 33553408 | bytes 34611200 | tf_op jit(solution)/shard_map/reduce_sum | solution.py:113
  442.6 0.0 copy-done
  442.6 14.0 %fusion.39 = bf16[64,8,128]{2,0,1:T(8,128)(2,1)S(1)} fusion(f32[8192,64,8]{0,1,2:T(8,128)} %get-tuple-element.17, f32[8,64]{1,0:T(8,128)S(1)} %log_add_fusion.1, pred[64,8192]{1,0:T(8,128)(4,1)S(1)} %get-tuple-element.10, bf16[8192,256]{1,0:T(8,128)(2,1)S(1)} %copy-done.3), kind=kOutput, calls=%fused_computation.40 | convolution fusion | flops 6455099392 | bytes 19533824 | tf_op jit(solution)/shard_map/hqk,kd->qhd/dot_general | solution.py:89
  456.6 0.1 copy.16
  456.7 0.1 concatenate.25
  456.8 14.7 %fusion.36 = bf16[64,8,128]{2,0,1:T(8,128)(2,1)S(1)} fusion(f32[8192,64,8]{0,1,2:T(8,128)} %copy-done, f32[8,64]{1,0:T(8,128)S(1)} %log_add_fusion, pred[64,8192]{1,0:T(8,128)(4,1)S(1)} %get-tuple-element.11, bf16[8192,256]{1,0:T(8,128)(2,1)} %all-gather.5.cloned.1.call-done), kind=kOutput, calls=%fused_computation.39 | convolution fusion | flops 6455099392 | bytes 19531776 | tf_op jit(solution)/shard_map/hqk,kd->qhd/dot_general | solution.py:89
  471.4 0.1 copy.18
  471.5 0.1 concatenate.26
  471.6 0.7 pad_maximum_fusion
  472.3 0.7 maximum_bitcast_fusion
  (10 shorter events, 0.1 us)
Async XLA Ops:
  7.2 284.7 %copy-start.2 = (bf16[1,128,1024]{2,1,0:T(8,128)(2,1)S(1)}, bf16[1,128,1024]{2,1,0:T(8,128)(2,1)}, u32[]{:S(2)}) copy-start(bf16[1,128,1024]{2,1,0:T(8,128)(2,1)} %param.8) | copy-start | bytes 786436
  10.5 276.2 %all-to-all-start = ((bf16[64,1,128,256]{3,2,1,0:T(8,128)(2,1)}), bf16[64,1,128,256]{3,2,1,0:T(8,128)(2,1)}, u32[]{:S(2)}, u32[]{:S(2)}) async-start(bf16[64,1,128,256]{3,2,1,0:T(8,128)(2,1)} %stack.2), calls=%async_computation | async-start | bytes 8388608 | tf_op jit(solution)/shard_map/all_to_all | solution.py:19
  28.0 256.7 %all-gather.3.cloned.1.call-start = ((), (), s32[]{:S(2)}) async-start(), calls=%async_computation.1 | async-start | bytes 2621440 | tf_op jit(solution)/shard_map/all_gather | solution.py:63
  28.0 107.8 %collective-permute-start = (bf16[1,128,2048]{2,1,0:T(8,128)(2,1)}, bf16[1,128,2048]{2,1,0:T(8,128)(2,1)S(1)}, u32[]{:S(2)}, u32[]{:S(2)}) collective-permute-start(bf16[1,128,2048]{2,1,0:T(8,128)(2,1)} %param.5), channel_id=1, source_target_pairs={{0,256},{256,0},{1,257},{257,1},{2,258},{258,2},{3,259},{259,3},{4... | collective-permute-start | bytes 1572872 | tf_op jit(solution)/shard_map/ppermute | solution.py:27
  135.8 0.8 copy-start.1
  136.7 278.7 %all-gather.5.cloned.1.call-start = ((), (), s32[]{:S(2)}) async-start(), calls=%async_computation.2 | async-start | bytes 4259840 | tf_op jit(solution)/shard_map/all_gather | solution.py:119
  415.4 4.8 copy-start.3
  420.2 22.4 %copy-start = (f32[8192,64,8]{0,1,2:T(8,128)}, f32[8192,64,8]{0,1,2:T(8,128)S(1)}, u32[]{:S(2)}) copy-start(f32[8192,64,8]{0,1,2:T(8,128)S(1)} %get-tuple-element.15) | copy-start | bytes 50331652
Sparse Core Ops, SparseCore 0:
  136.8 147.8 all-gather.2
  292.0 123.3 all-gather.4
